TPU v7x, 256 devices: a whole 4x4x8 slice. The times are simulated.
256 devices in a mesh: outer: 16 (over y, x), inner: 16 (over z, core).
Axes of the slice: x: 4, y: 4, z: 8, core: 2. Of those that a mesh axis runs over, the one named last changes fastest.
Arguments:
- tokens: bfloat16 [98304, 1024], P(('outer', 'inner')), may hold values from -6 to 6
- log_decay: float32 [98304, 16], P(('outer', 'inner')), may hold values from -1 to 0, as said below
- query_weight: bfloat16 [1024, 1024], replicated, may hold values from -0.1875 to 0.1875
- key_weight: bfloat16 [1024, 1024], replicated, may hold values from -0.1875 to 0.1875
- value_weight: bfloat16 [1024, 1024], replicated, may hold values from -0.1875 to 0.1875
- norm_gain: float32 [1024], replicated, may hold values from 0.1 to 1.9
- output_weight: bfloat16 [1024, 1024], replicated, may hold values from -0.1875 to 0.1875
Outputs:
- mixed: bfloat16 [98304, 1024], P(('outer', 'inner'))
Inputs may be any that keep to these rules, and one draw needn't show every extreme that they name: log_decay is negative.
All inputs are finite; a program needn't handle non-finite values.
Results may differ from a plain program's by a relative error of at most 0.0063.
Values sent between devices are 32-bit elements; how exact they have to be, the bound alone decides.
A program may use at most 320 MiB of HBM per device.

v0:
```python
import jax
import jax.numpy as jnp
from jax import lax
from jax.sharding import PartitionSpec as P


def prefix(value, axis, join, neutral):
    count, mine = (lax.axis_size(axis), lax.axis_index(axis))
    pieces = jax.tree.map(lambda part: lax.all_gather(part, axis), value)
    running = jax.tree.map(
        lambda part, zero: jnp.full_like(part, 0) + jnp.asarray(zero, part.dtype), value, neutral
    )

    def lap(position, running):
        longer = join(running, jax.tree.map(lambda part: part[position], pieces))
        return jax.tree.map(lambda new, old: jnp.where(position < mine, new, old), longer, running)

    return lax.fori_loop(0, count - 1, lap, running)


def broadcast(value, axis, source):
    kept = jnp.where(lax.axis_index(axis) == source, value, 0).astype(value.dtype)
    return lax.psum(kept, axis)


def local_head(q_head, k_head, v_head, g_head):
    cum = jnp.cumsum(g_head)
    count = cum.shape[0]
    rows = lax.broadcasted_iota(jnp.int32, (count, count), 0)
    cols = lax.broadcasted_iota(jnp.int32, (count, count), 1)
    lower = cols <= rows
    diff = jnp.where(lower, cum[:, None] - cum[None, :], 0.0)
    decay = jnp.where(lower, jnp.exp(diff), 0.0)
    scores = jnp.dot(q_head, k_head.T, preferred_element_type=jnp.float32)
    weights = (scores * decay).astype(jnp.bfloat16)
    intra = jnp.dot(weights, v_head, preferred_element_type=jnp.float32)
    last = cum[-1]
    scaled = (k_head.astype(jnp.float32) * jnp.exp(last - cum)[:, None]).astype(jnp.bfloat16)
    local = jnp.dot(scaled.T, v_head, preferred_element_type=jnp.float32)
    return (intra, local, jnp.exp(last))


def combine(earlier, later):
    return (earlier[0] * later[0], later[0][:, None, None] * earlier[1] + later[1])


def shards(tokens, log_decay, query_weight, key_weight, value_weight, norm_gain, output_weight):
    count = tokens.shape[0]
    heads = log_decay.shape[1]
    queries = jax.nn.silu(jnp.dot(tokens, query_weight, preferred_element_type=jnp.float32)).astype(
        jnp.bfloat16
    )
    keys = jax.nn.silu(jnp.dot(tokens, key_weight, preferred_element_type=jnp.float32)).astype(
        jnp.bfloat16
    )
    value_rows = jnp.dot(tokens, value_weight, preferred_element_type=jnp.float32).astype(
        jnp.bfloat16
    )
    split = lambda arr: arr.reshape(count, heads, -1).transpose(1, 0, 2)
    queries, keys, value_rows = (split(queries), split(keys), split(value_rows))
    intra, local, fall = lax.map(
        lambda token_parts: local_head(*token_parts), (queries, keys, value_rows, log_decay.T)
    )
    own = (fall, local)
    identity = (jnp.ones_like(fall), jnp.zeros_like(local))
    inner_before = prefix(own, "inner", combine, identity)
    inclusive = combine(inner_before, own)
    total = (
        broadcast(inclusive[0], "inner", lax.axis_size("inner") - 1),
        broadcast(inclusive[1], "inner", lax.axis_size("inner") - 1),
    )
    outer_before = prefix(total, "outer", combine, identity)
    incoming = combine(outer_before, inner_before)[1]
    cum = jnp.cumsum(log_decay, axis=0)
    qfloat = queries.astype(jnp.float32)
    inter = (
        jnp.einsum("htd,hde->the", qfloat, incoming, precision=lax.Precision.HIGHEST)
        * jnp.exp(cum)[:, :, None]
    )
    attended = intra.transpose(1, 0, 2) + inter
    scale = lax.rsqrt(jnp.mean(attended * attended, axis=-1, keepdims=True) + 1e-05)
    normalized_output = ((attended * scale).reshape(count, -1) * norm_gain).astype(jnp.bfloat16)
    return jnp.dot(normalized_output, output_weight, preferred_element_type=jnp.float32).astype(
        jnp.bfloat16
    )


def solution(mesh):
    in_specs = (P(("outer", "inner"), None), P(("outer", "inner"), None), P(), P(), P(), P(), P())
    out_specs = P(("outer", "inner"), None)
    return jax.shard_map(shards, mesh=mesh, in_specs=in_specs, out_specs=out_specs, check_vma=False)
```

profile of v0, /device:TPU:25, one launch (start us, length us, event | category | flops | bytes accessed | tf_op | source)
XLA Modules:
  0.0 438.9 jit_solution(5234878555848884277)
XLA Ops:
  8.1 3.2 multiply_convert_fusion.2
  12.8 3.9 multiply_convert_fusion.1
  16.7 2.3 copy.24
  18.9 3.7 convolution_convert_fusion.1
  22.6 2.3 copy.25
  25.0 115.7 %while.47 = (s32[]{:T(128)}, f32[16,384,64]{1,2,0:T(8,128)}, f32[16,64,64]{2,1,0:T(8,128)}, f32[16]{0:T(128)S(1)}, bf16[16,384,64]{1,2,0:T(8,128)(2,1)S(1)}, /*i...) while((s32[]{:T(128)}, f32[16,384,64]{1,2,0:T(8,128)}, ...), condition=%wide.region_3.4_spmd.clone, body=%wide.region_0.3_spmd.sunk.clone | while | flops 41902472 | bytes 594653 | solution.py:61
  29.5 1.9 fusion.74
  43.9 1.9 fusion.74
  51.2 1.9 fusion.74
  58.4 1.9 fusion.74
  80.1 1.9 fusion.74
  87.3 1.9 fusion.74
  94.6 1.9 fusion.74
  137.9 1.9 fusion.74
  142.2 27.6 %all-reduce = f32[256]{0:T(256)S(1)} all-reduce(f32[256]{0:T(256)S(1)} %dynamic-update-slice), channel_id=2, replica_groups=mesh['outer'=16,'inner'=16] {'inner'}, use_global_device_ids=true, to_apply=%add | all-reduce | flops 256 | bytes 2048
  169.9 30.2 %all-gather.8.cloned.1.call-done = f32[256,64,64]{2,1,0:T(8,128)} async-done(((f32[16,64,64]{2,1,0:T(8,128)}), f32[256,64,64]{2,1,0:T(8,128)}) %all-gather.8.cloned.1.call-update) | async-done | bytes 4194320 | tf_op jit(solution)/shard_map/all_gather | solution.py:9
  200.1 18.3 %while.48 = (s32[]{:T(128)}, f32[16]{0:T(128)S(1)}, f32[16,64,64]{2,1,0:T(8,128)S(1)}, s32[]{:T(128)}, f32[16,16]{1,0:T(8,128)S(1)}, /*index=5*/f32[16,16,64,64]{3,2,1,0:T(8,128)}) while((s32[]{:T(128)}, f32[16]{0:T(128)S(1)}, f32[16,64,64]{2,1,0:T(8,128)S(1)}, s32[]{:T(128)}, f32[16,16]{1,0:T(8,128)S(1)}, ...), condition=%wide.region_5.6_spmd.clone.clone, body=%wide.region_4.5_spmd.clone.sunk.clone | while | flops 262196 | bytes 786851 | solution.py:18
  218.4 2.0 select_bitcast_fusion
  220.4 107.8 %all-reduce.3.cloned.1.call-done = f32[1,16,64,64]{3,2,1,0:T(8,128)} async-done(((f32[1,16,64,64]{3,2,1,0:T(8,128)}), f32[1,16,64,64]{3,2,1,0:T(8,128)}) %all-reduce.3.cloned.1.call-update) | async-done | bytes 262160 | tf_op jit(solution)/shard_map/psum | solution.py:23
  329.4 24.0 %psum.14 = f32[1,16]{1,0:T(1,128)S(1)} all-reduce(f32[1,16]{1,0:T(1,128)S(1)} %fusion.37), channel_id=1, replica_groups=mesh['outer'=16,'inner'=16] {'inner'}, use_global_device_ids=true, to_apply=%region_6.7 | all-reduce | flops 16 | bytes 128 | tf_op jit(solution)/shard_map/psum | solution.py:23
  353.4 15.0 %all-gather.2 = f32[16,1,16]{2,1,0:T(1,128)S(1)} all-gather(f32[1,1,16]{2,1,0:T(1,128)S(1)} %bitcast.147), channel_id=1, replica_groups=mesh['outer'=16,'inner'=16] {'outer'}, dimensions={0}, use_global_device_ids=true | all-gather | bytes 1088 | tf_op jit(solution)/shard_map/all_gather | solution.py:9
  368.4 38.6 %all-gather.6.cloned.1.call-done = f32[16,16,64,64]{3,2,1,0:T(8,128)} async-done(((f32[1,16,64,64]{3,2,1,0:T(8,128)}), f32[16,16,64,64]{3,2,1,0:T(8,128)}) %all-gather.6.cloned.1.call-update) | async-done | bytes 4194320 | tf_op jit(solution)/shard_map/all_gather | solution.py:9
  407.1 18.2 %while.49 = (s32[]{:T(128)}, f32[16,64,64]{2,1,0:T(8,128)S(1)}, s32[]{:T(128)}, f32[16,16]{1,0:T(8,128)S(1)}, f32[16,16,64,64]{3,2,1,0:T(8,128)}) while((s32[]{:T(128)}, f32[16,64,64]{2,1,0:T(8,128)S(1)}, s32[]{:T(128)}, f32[16,16]{1,0:T(8,128)S(1)}, f32[16,16,64,64]{3,2,1,0:T(8,128)}) %tuple.108), condition=%wide.region_9.10_spmd.clone.clone, body=%wide.region_8.9_spmd.clone.sunk.clone | while | flops 262148 | bytes 786713 | solution.py:18
  425.3 2.9 multiply_reduce_fusion
  (299 shorter events, 134.2 us)
Async XLA Ops:
  6.5 1.6 copy-start
  6.5 193.5 %all-gather.8.cloned.1.call-start = ((), (), s32[]{:S(2)}) async-start(), calls=%async_computation.2 | async-start | bytes 8912896 | tf_op jit(solution)/shard_map/all_gather | solution.py:9
  22.6 2.3 copy-start.3
  25.0 115.8 %copy-start.5 = (u32[256]{0:T(256)S(1)}, u32[256]{0:T(256)}, u32[]{:S(2)}) copy-start(u32[256]{0:T(256)} %constant.98) | copy-start | bytes 3076
  140.7 79.7 %copy-start.1 = (bf16[16,384,64]{1,2,0:T(8,128)(2,1)}, bf16[16,384,64]{1,2,0:T(8,128)(2,1)S(1)}, u32[]{:S(2)}) copy-start(bf16[16,384,64]{1,2,0:T(8,128)(2,1)S(1)} %get-tuple-element.586) | copy-start | bytes 2359300
  140.7 187.5 %all-reduce.3.cloned.1.call-start = ((), (), s32[]{:S(2)}) async-start(), calls=%async_computation | async-start | bytes 1048576 | tf_op jit(solution)/shard_map/psum | solution.py:23
  220.4 186.7 %all-gather.6.cloned.1.call-start = ((), (), s32[]{:S(2)}) async-start(), calls=%async_computation.1 | async-start | bytes 8912896 | tf_op jit(solution)/shard_map/all_gather | solution.py:9
  428.2 0.7 copy-start.4
  428.8 1.6 copy-start.2
Sparse Core Ops, SparseCore 0:
  140.8 59.2 all-gather.7
  220.5 107.6 all-reduce.2
  330.9 76.0 all-gather.5
where the time goes:
time: 445 us; the launch traced here: 439 us
  waiting for transfers between devices  177 us (40%)
  matrix products  73.1 us (16%)
  blocking collectives  66.6 us (15%)
  other arithmetic  55.9 us (13%)
  local copies, waits for them, and re-layouts  40.5 us (9%)
  between operations  13.8 us (3%)
  loops' own time  12.1 us (3%)
    psum x1, waiting for transfers between devices, broadcast(): return lax.psum(kept, axis)  108 us
    all_gather x2, waiting for transfers between devices, prefix(): pieces = jax.tree.map(lambda part: lax.all_gather(part, axis), value)  68.9 us
    select_n x45, other arithmetic, lap(): jnp.where(position < mine, new, old)  35.5 us
    dot_general x16, matrix products, local_head(): intra = jnp.dot(weights, v_head, preferred_element_type=jnp.float32)  30.6 us
    unnamed x1, blocking collectives  27.6 us
    dot_general x16, matrix products, local_head(): local = jnp.dot(scaled.T, v_head, preferred_element_type=jnp.float32)  27 us
    psum x1, blocking collectives, broadcast(): return lax.psum(kept, axis)  24 us
    dynamic_slice x48, local copies, waits for them, and re-layouts, shards(): lax.map(lambda token_parts: local_head(*token_parts), (queries, keys, val...  15.3 us
  transfers between devices with their start and end apart: 3, of which 3 were waited for; matrix products, arithmetic and copies ran while one was open for 0% of the time, Pallas kernels for 0%

commit v1 on v0

v1 whole, which is shorter than its diff:
```python
import functools

import jax
import jax.numpy as jnp
from jax import lax
from jax.experimental import pallas as pl
from jax.experimental.pallas import tpu as pltpu
from jax.sharding import PartitionSpec as P

F32 = jnp.float32
BF16 = jnp.bfloat16
HEADS = 16
HEAD = 64
PAIRS = 8
PAIR = 128
QUADS = 4
QUAD = 256
TOKENS = 384
SUB = 128
WIDTH = 1024
HALF = 32


def dot(a, b):
    return jnp.dot(a, b, preferred_element_type=F32)


def dot_nt(a, b):
    return lax.dot_general(a, b, (((1,), (1,)), ((), ())), preferred_element_type=F32)


def dot_tn(a, b):
    return lax.dot_general(a, b, (((0,), (0,)), ((), ())), preferred_element_type=F32)


def silu(x):
    return x * (0.5 * jnp.tanh(0.5 * x) + 0.5)


def split3(x):
    hi = x.astype(BF16)
    rest = x - hi.astype(F32)
    mid = rest.astype(BF16)
    return hi, mid, (rest - mid.astype(F32)).astype(BF16)


def kernel(
    outers,
    chips,
    tok_hbm,
    decay_hbm,
    wq_hbm,
    wk_hbm,
    wv_hbm,
    gain_hbm,
    wo_hbm,
    out_hbm,
    tok,
    decay,
    wq,
    wk,
    wv,
    gain,
    wo,
    q,
    k,
    v,
    cum_b,
    cum_t,
    intra,
    local,
    crossed,
    chip,
    in1,
    prefix,
    total,
    in2,
    out3,
    in3,
    give,
    state,
    f_own,
    f_sib,
    f_chip,
    f_in1,
    f_group,
    f_in2,
    normed,
    out,
    load_sem,
    store_sem,
    f0_sem,
    f1_sem,
    f2_sem,
    s0_sem,
    s1_sem,
    s2_sem,
    s3_sem,
    s4_sem,
):
    o = lax.axis_index("outer")
    inner = lax.axis_index("inner")
    z, c = inner // 2, inner % 2
    sibling = (o, z * 2 + 1 - c)

    def along(d):
        return (z + d) % chips

    def at_z(other):
        return (o, other * 2 + c)

    def at_o(other):
        return (other, inner)

    def load(src, dst, n):
        copy = pltpu.make_async_copy(src, dst, load_sem.at[n])
        copy.start()
        return copy

    load_decay = load(decay_hbm, decay, 0)
    load_tok = load(tok_hbm, tok, 1)
    load_k, load_v, load_q, load_o = [], [], [], []
    for n in range(QUADS):
        cols = pl.ds(n * QUAD, QUAD)
        load_k.append(load(wk_hbm.at[:, cols], wk.at[n], 2 + n))
        load_v.append(load(wv_hbm.at[:, cols], wv.at[n], 6 + n))
    for n in range(QUADS):
        cols = pl.ds(n * QUAD, QUAD)
        load_q.append(load(wq_hbm.at[:, cols], wq.at[n], 10 + n))
    for n in range(QUADS):
        cols = pl.ds(n * QUAD, QUAD)
        load_o.append(load(wo_hbm.at[:, cols], wo.at[n], 14 + n))
    load_gain = load(gain_hbm, gain, 18)

    barrier = pltpu.get_barrier_semaphore()
    pl.semaphore_signal(barrier, inc=1, device_id=sibling, device_id_type=MESH)
    for d in range(1, chips):
        pl.semaphore_signal(barrier, inc=1, device_id=at_z(along(d)), device_id_type=MESH)
    for d in range(1, outers):
        pl.semaphore_signal(barrier, inc=1, device_id=at_o((o + d) % outers), device_id_type=MESH)

    sent = []

    def send(src, dst, sems, slot_out, slot_in, device):
        copy = pltpu.make_async_remote_copy(
            src_ref=src,
            dst_ref=dst,
            send_sem=sems.at[0, slot_out],
            recv_sem=sems.at[1, slot_in],
            device_id=device,
            device_id_type=MESH,
        )
        copy.start()
        return copy

    def arrived(dst, sems, slot_in):
        pltpu.make_async_remote_copy(
            src_ref=dst,
            dst_ref=dst,
            send_sem=sems.at[0, slot_in],
            recv_sem=sems.at[1, slot_in],
            device_id=sibling,
            device_id_type=MESH,
        ).wait_recv()

    lane = lax.broadcasted_iota(jnp.int32, (1, PAIR), 1)
    first = lane < HEAD
    rows = lax.broadcasted_iota(jnp.int32, (TOKENS, TOKENS), 0)
    cols = lax.broadcasted_iota(jnp.int32, (TOKENS, TOKENS), 1)
    triangle = jnp.where(cols <= rows, 1.0, 0.0).astype(BF16)
    load_decay.wait()
    hi, mid, lo = split3(decay[...])
    cum = dot(triangle, hi) + (dot(triangle, mid) + dot(triangle, lo))
    for h in range(HEADS):
        cum_b[h] = jnp.broadcast_to(cum[:, h : h + 1], (TOKENS, PAIR))
    wide = jnp.concatenate([cum, jnp.zeros((TOKENS, PAIR - HEADS), F32)], axis=1)
    turned = wide.T
    for h in range(HEADS):
        cum_t[h] = turned[h : h + 1, :]

    def pair_cum(p):
        return jnp.where(first, cum_b[2 * p], cum_b[2 * p + 1])

    for p in range(PAIRS):
        last = jnp.where(
            first, cum_b[2 * p, TOKENS - 1 : TOKENS, :], cum_b[2 * p + 1, TOKENS - 1 : TOKENS, :]
        )
        f_own[p : p + 1, :] = jnp.exp(last)

    pl.semaphore_wait(barrier, chips + outers - 1)
    sent.append(send(f_own, f_sib, f0_sem, 0, 0, sibling))

    load_tok.wait()
    for n in range(QUADS):
        load_k[n].wait()
        keys = silu(dot(tok[...], wk[n])).astype(BF16)
        load_v[n].wait()
        values = dot(tok[...], wv[n]).astype(BF16)
        for e in range(2):
            p = 2 * n + e
            part = slice(e * PAIR, (e + 1) * PAIR)
            k[p] = keys[:, part]
            v[p] = values[:, part]
            run = pair_cum(p)
            left = jnp.exp(run[TOKENS - 1 :, :] - run)
            scaled = (keys[:, part].astype(F32) * left).astype(BF16)
            outer = dot_tn(scaled, values[:, part])
            own = jnp.where(first, outer[:HEAD], outer[HEAD:])
            local[p] = own.reshape(2, HALF, PAIR)
        two = pl.ds(2 * n, 2)
        sent.append(send(local.at[two, 1 - c], crossed.at[two], s0_sem, n, n, sibling))

    arrived(f_sib, f0_sem, 0)
    fall0 = jnp.where(c == 0, f_own[...], f_sib[...])
    fall1 = jnp.where(c == 0, f_sib[...], f_own[...])
    f_chip[...] = fall0 * fall1
    f_in1[z] = fall0 * fall1
    for d in range(1, chips):
        sent.append(send(f_chip, f_in1.at[z], f1_sem, d, z, at_z(along(d))))

    def project_queries(n):
        load_q[n].wait()
        queries = silu(dot(tok[...], wq[n])).astype(BF16)
        q[2 * n] = queries[:, :PAIR]
        q[2 * n + 1] = queries[:, PAIR:]

    def attend(p):
        def head(e):
            keep = first if e == 0 else jnp.logical_not(first)
            h = 2 * p + e
            pieces = []
            for i in range(TOKENS // SUB):
                here = pl.ds(i * SUB, SUB)
                upto = (i + 1) * SUB
                mine = jnp.where(keep, q[p, here, :].astype(F32), 0.0).astype(BF16)
                scores = dot_nt(mine, k[p, :upto, :])
                row = cum_b[h, here, :]
                blocks = []
                for j in range(i + 1):
                    diff = row - cum_t[h, :, j * SUB : (j + 1) * SUB]
                    if j == i:
                        r = lax.broadcasted_iota(jnp.int32, (SUB, SUB), 0)
                        s = lax.broadcasted_iota(jnp.int32, (SUB, SUB), 1)
                        diff = jnp.where(s <= r, diff, -jnp.inf)
                    blocks.append(
                        (scores[:, j * SUB : (j + 1) * SUB] * jnp.exp(diff)).astype(BF16)
                    )
                weights = jnp.concatenate(blocks, axis=1)
                pieces.append(dot(weights, v[p, :upto, :]))
            return pieces

        for i, (one, two) in enumerate(zip(head(0), head(1))):
            intra[p, i * SUB : (i + 1) * SUB, :] = jnp.where(first, one, two)

    def attend_pairs(start, stop):
        def body(p, carry):
            attend(p)
            return carry

        lax.fori_loop(start, stop, body, 0)

    for n in range(QUADS):
        project_queries(n)

    for n in range(QUADS):
        arrived(crossed.at[pl.ds(2 * n, 2)], s0_sem, n)
    for p in range(PAIRS):
        mine = local[p, c]
        theirs = crossed[p]
        f1 = fall1[p : p + 1, :]
        chip[p] = jnp.where(c == 0, f1 * mine + theirs, f1 * theirs + mine)
    in1[z] = chip[z]
    for d in range(1, chips):
        t = along(d)
        sent.append(send(chip.at[t], in1.at[z], s1_sem, d, z, at_z(t)))

    for d in range(1, chips):
        arrived(f_in1.at[along(d)], f1_sem, along(d))
    group = f_in1[0]
    for i in range(1, chips):
        group = group * f_in1[i]
    f_group[...] = group
    later = []
    for d in range(1, outers):

        def go(d=d):
            send(f_group, f_in2.at[o], f2_sem, d, o, at_o(o + d))

        pl.when(o + d < outers)(go)

    attend_pairs(0, 2)

    for d in range(1, chips):
        arrived(in1.at[along(d)], s1_sem, along(d))
    run = jnp.zeros((HALF, PAIR), F32)
    for i in range(chips):
        prefix[i] = run
        run = f_in1[i, pl.ds(z, 1), :] * run + in1[i]
    total[...] = run
    for d in range(1, outers):

        def go(d=d):
            send(total, in2.at[o], s2_sem, d, o, at_o(o + d))

        pl.when(o + d < outers)(go)

    attend_pairs(2, 4)

    def earlier(i, before):
        arrived(f_in2.at[i], f2_sem, i)
        arrived(in2.at[i], s2_sem, i)
        return f_in2[i, pl.ds(z, 1), :] * before + in2[i]

    before = lax.fori_loop(0, o, earlier, jnp.zeros((HALF, PAIR), F32))
    fall = jnp.ones((1, PAIR), F32)
    for i in range(chips):
        out3[i] = fall * before + prefix[i]
        fall = fall * f_in1[i, pl.ds(z, 1), :]
    in3[z] = out3[z]
    for d in range(1, chips):
        t = along(d)
        sent.append(send(out3.at[t], in3.at[z], s3_sem, d, z, at_z(t)))

    attend_pairs(4, 8)

    for d in range(0, chips):
        p = along(d)
        if d > 0:
            arrived(in3.at[p], s3_sem, p)
        enters = in3[p]
        first_local = jnp.where(c == 0, local[p, 0], crossed[p])
        f0 = jnp.where(c == 0, f_own[pl.ds(p, 1), :], f_sib[pl.ds(p, 1), :])
        middle = f0 * enters + first_local
        state[p, c] = jnp.where(c == 0, enters, middle)
        give[p] = jnp.where(c == 0, middle, enters)
        sent.append(send(give.at[p], state.at[p, c], s4_sem, p, p, sibling))

    load_gain.wait()
    r = lax.broadcasted_iota(jnp.int32, (PAIR, PAIR), 0) // HEAD
    s = lax.broadcasted_iota(jnp.int32, (PAIR, PAIR), 1) // HEAD
    means = jnp.where(r == s, 1.0 / HEAD, 0.0).astype(BF16)
    for p in range(PAIRS):
        arrived(state.at[p, 1 - c], s4_sem, p)
        flat = state[p].reshape(HEAD, PAIR)
        both = jnp.concatenate([jnp.where(first, flat, 0.0), jnp.where(first, 0.0, flat)], axis=0)
        hi = both.astype(BF16)
        lo = (both - hi.astype(F32)).astype(BF16)
        inter = dot(q[p], hi) + dot(q[p], lo)
        attended = intra[p] + jnp.exp(pair_cum(p)) * inter
        mean = dot((attended * attended).astype(BF16), means)
        part = slice(p * PAIR, (p + 1) * PAIR)
        normed[:, part] = (attended * lax.rsqrt(mean + 1e-5) * gain[:, part]).astype(BF16)

    stores = []
    for n in range(QUADS):
        load_o[n].wait()
        out[n] = dot(normed[...], wo[n]).astype(BF16)
        copy = pltpu.make_async_copy(
            out.at[n], out_hbm.at[:, pl.ds(n * QUAD, QUAD)], store_sem.at[n]
        )
        copy.start()
        stores.append(copy)

    for copy in sent:
        copy.wait_send()
    for d in range(1, outers):

        def finish(d=d):
            for src, sems in ((f_group, f2_sem), (total, s2_sem)):
                pltpu.make_async_remote_copy(
                    src_ref=src,
                    dst_ref=src,
                    send_sem=sems.at[0, d],
                    recv_sem=sems.at[1, d],
                    device_id=sibling,
                    device_id_type=MESH,
                ).wait_send()

        pl.when(o + d < outers)(finish)
    for copy in stores:
        copy.wait()


MESH = pl.DeviceIdType.MESH


def solution(mesh):
    outers, chips = mesh.shape["outer"], mesh.shape["inner"] // 2

    def shards(tokens, log_decay, query_weight, key_weight, value_weight, norm_gain, output_weight):
        vmem = pltpu.VMEM
        dma = pltpu.SemaphoreType.DMA
        weight = vmem((QUADS, WIDTH, QUAD), BF16)
        by_pair = vmem((PAIRS, TOKENS, PAIR), BF16)
        unit = (HALF, PAIR)
        tile = (PAIRS, PAIR)
        return pl.pallas_call(
            functools.partial(kernel, outers, chips),
            out_shape=jax.ShapeDtypeStruct((TOKENS, WIDTH), BF16),
            in_specs=[pl.BlockSpec(memory_space=pl.ANY)] * 7,
            out_specs=pl.BlockSpec(memory_space=pl.ANY),
            scratch_shapes=[
                vmem((TOKENS, WIDTH), BF16),
                vmem((TOKENS, HEADS), F32),
                weight,
                weight,
                weight,
                vmem((1, WIDTH), F32),
                weight,
                by_pair,
                by_pair,
                by_pair,
                vmem((HEADS, TOKENS, PAIR), F32),
                vmem((HEADS, 1, TOKENS), F32),
                vmem((PAIRS, TOKENS, PAIR), F32),
                vmem((PAIRS, 2) + unit, F32),
                vmem((PAIRS,) + unit, F32),
                vmem((PAIRS,) + unit, F32),
                vmem((chips,) + unit, F32),
                vmem((chips,) + unit, F32),
                vmem(unit, F32),
                vmem((outers,) + unit, F32),
                vmem((chips,) + unit, F32),
                vmem((PAIRS,) + unit, F32),
                vmem((PAIRS,) + unit, F32),
                vmem((PAIRS, 2) + unit, F32),
                vmem(tile, F32),
                vmem(tile, F32),
                vmem(tile, F32),
                vmem((chips,) + tile, F32),
                vmem(tile, F32),
                vmem((outers,) + tile, F32),
                vmem((TOKENS, WIDTH), BF16),
                vmem((QUADS, TOKENS, QUAD), BF16),
                dma((19,)),
                dma((QUADS,)),
                dma((2, 1)),
                dma((2, chips)),
                dma((2, outers)),
                dma((2, QUADS)),
                dma((2, chips)),
                dma((2, outers)),
                dma((2, chips)),
                dma((2, PAIRS)),
            ],
            compiler_params=pltpu.CompilerParams(
                collective_id=0, has_side_effects=True, vmem_limit_bytes=48 << 20
            ),
            cost_estimate=pl.CostEstimate(
                flops=4 * 10**9, bytes_accessed=10 << 20, transcendentals=2 * 10**6
            ),
        )(
            tokens,
            log_decay,
            query_weight,
            key_weight,
            value_weight,
            norm_gain.reshape(1, WIDTH),
            output_weight,
        )

    in_specs = (P(("outer", "inner"), None), P(("outer", "inner"), None), P(), P(), P(), P(), P())
    out_specs = P(("outer", "inner"), None)
    return jax.shard_map(shards, mesh=mesh, in_specs=in_specs, out_specs=out_specs, check_vma=False)
```

time: 445 us -> 48 us (0.11); the launches traced: 439 us -> 47.8 us
  waiting for transfers between devices: 177 us -> 0 us
  matrix products: 73.1 us -> 0 us
  blocking collectives: 66.6 us -> 0 us
  other arithmetic: 55.9 us -> 0 us
  Pallas kernels: 0 us -> 41 us
  local copies, waits for them, and re-layouts: 40.5 us -> 6.74 us
  between operations: 13.8 us -> 0.03 us
  loops' own time: 12.1 us -> 0 us
    psum x1 -> x0, waiting for transfers between devices: 108 us -> none  [broadcast(): return lax.psum(kept, axis)]
    dot_general x37 -> x0, matrix products: 73.1 us -> none  [the longest x16 30.6 us: local_head(): intra = jnp.dot(weights, v_head, preferred_element_type=jnp.float32)]
    all_gather x2 -> x0, waiting for transfers between devices: 68.9 us -> none  [prefix(): pieces = jax.tree.map(lambda part: lax.all_gather(part, axis), value)]
    pallas_call x0 -> x1, Pallas kernels: none -> 41 us  [shards(): pl.pallas_call(functools.partial(kernel, outers, chips), out_shape=jax.Sh...]
    select_n x45 -> x0, other arithmetic: 35.5 us -> none  [lap(): jnp.where(position < mine, new, old)]
    unnamed x1 -> x0, blocking collectives: 27.6 us -> none
    psum x1 -> x0, blocking collectives: 24 us -> none  [broadcast(): return lax.psum(kept, axis)]
    dynamic_slice x48 -> x0, local copies, waits for them, and re-layouts: 15.3 us -> none  [shards(): lax.map(lambda token_parts: local_head(*token_parts), (queries, keys, val...]
  transfers between devices with their start and end apart: 3 -> 0, of which waited for: 3 -> 0; matrix products, arithmetic and copies ran while one was open for 0% -> 0% of each run, Pallas kernels for 0% -> 0%
where the time goes in v1:
time: 48 us; the launch traced here: 47.8 us
  Pallas kernels  41 us (85%)
  local copies, waits for them, and re-layouts  6.74 us (14%)
    pallas_call x1, Pallas kernels, shards(): pl.pallas_call(functools.partial(kernel, outers, chips), out_shape=jax.Sh...  41 us
    unnamed x10, local copies, waits for them, and re-layouts  6.74 us

profile of v1, /device:TPU:25, one launch (start us, length us, event | category | flops | bytes accessed | tf_op | source)
XLA Modules:
  0.0 47.8 jit_solution(6529056537233811460)
XLA Ops:
  0.0 0.9 %copy.8.decay_hbm = f32[384,16]{1,0:T(8,128)S(1)} copy(f32[384,16]{0,1:T(8,128)} %param.8) | data formatting | bytes 49152 | tf_op args[1]
  0.9 0.0 copy-start
  0.9 1.6 %copy-done = bf16[1024,1024]{1,0:T(8,128)(2,1)S(1)} copy-done((bf16[1024,1024]{1,0:T(8,128)(2,1)S(1)}, bf16[1024,1024]{1,0:T(8,128)(2,1)}, u32[]{:S(2)}) %copy-start) | copy-done | bytes 2097176
  2.5 0.0 copy-start.1
  2.5 1.6 %copy-done.1 = bf16[1024,1024]{1,0:T(8,128)(2,1)S(1)} copy-done((bf16[1024,1024]{1,0:T(8,128)(2,1)S(1)}, bf16[1024,1024]{1,0:T(8,128)(2,1)}, u32[]{:S(2)}) %copy-start.1) | copy-done | bytes 2097176
  4.1 0.0 copy-start.2
  4.1 1.1 %copy-done.2 = bf16[384,1024]{1,0:T(8,128)(2,1)S(1)} copy-done((bf16[384,1024]{1,0:T(8,128)(2,1)S(1)}, bf16[384,1024]{1,0:T(8,128)(2,1)}, u32[]{:S(2)}) %copy-start.2) | copy-done | bytes 786456
  5.2 0.0 copy-start.3
  5.2 0.7 %copy-done.3 = f32[1024]{0:T(1024)S(1)} copy-done((f32[1024]{0:T(1024)S(1)}, f32[1024]{0:T(1024)}, u32[]{:S(2)}) %copy-start.3) | copy-done | bytes 4120
  5.9 41.0 %shard_map.73 = bf16[384,1024]{1,0:T(8,128)(2,1)S(1)} custom-call(bf16[384,1024]{1,0:T(8,128)(2,1)S(1)} %copy-done.2, f32[384,16]{1,0:T(8,128)S(1)} %copy.8.decay_hbm, bf16[1024,1024]{1,0:T(8,128)(2,1)S(1)} %copy-done, bf16[1024,1024]{1,0:T(8,128)(2,1)S(1)} %copy-done.1, bf16[1024,1024]{1,0:T(8,128)(2,1)} %wv_hbm.1, f32[1,1024]{1,0:T(1,128)S(1)} %bitcast.1, ...), custom_call_target="tpu_custom_call" | custom-call | flops 4000000000 | bytes 10485760 | tf_op jit(solution)/shard_map/pallas_call | solution.py:397
  46.9 0.9 %copy.10 = bf16[384,1024]{1,0:T(8,128)(2,1)} copy(bf16[384,1024]{1,0:T(8,128)(2,1)S(1)} %shard_map.73) | data formatting | bytes 1572864
Async XLA Ops:
  0.9 1.6 %copy-start = (bf16[1024,1024]{1,0:T(8,128)(2,1)S(1)}, bf16[1024,1024]{1,0:T(8,128)(2,1)}, u32[]{:S(2)}) copy-start(bf16[1024,1024]{1,0:T(8,128)(2,1)} %wq_hbm.1) | copy-start | bytes 6291460
  2.5 1.6 %copy-start.1 = (bf16[1024,1024]{1,0:T(8,128)(2,1)S(1)}, bf16[1024,1024]{1,0:T(8,128)(2,1)}, u32[]{:S(2)}) copy-start(bf16[1024,1024]{1,0:T(8,128)(2,1)} %wk_hbm.1) | copy-start | bytes 6291460
  4.1 1.1 %copy-start.2 = (bf16[384,1024]{1,0:T(8,128)(2,1)S(1)}, bf16[384,1024]{1,0:T(8,128)(2,1)}, u32[]{:S(2)}) copy-start(bf16[384,1024]{1,0:T(8,128)(2,1)} %tok_hbm.1) | copy-start | bytes 2359300
  5.2 0.7 %copy-start.3 = (f32[1024]{0:T(1024)S(1)}, f32[1024]{0:T(1024)}, u32[]{:S(2)}) copy-start(f32[1024]{0:T(1024)} %param.12) | copy-start | bytes 12292

commit v2 on v1

v2 whole, which is shorter than its diff:
```python
import functools

import jax
import jax.numpy as jnp
from jax import lax
from jax.experimental import pallas as pl
from jax.experimental.pallas import tpu as pltpu
from jax.sharding import PartitionSpec as P

F32 = jnp.float32
BF16 = jnp.bfloat16
HEADS = 16
HEAD = 64
PAIRS = 8
PAIR = 128
QUADS = 4
QUAD = 256
TOKENS = 384
SUB = 128
WIDTH = 1024
SIDE = 4
HALF = 32


def dot(a, b):
    return jnp.dot(a, b, preferred_element_type=F32)


def dot_nt(a, b):
    return lax.dot_general(a, b, (((1,), (1,)), ((), ())), preferred_element_type=F32)


def dot_tn(a, b):
    return lax.dot_general(a, b, (((0,), (0,)), ((), ())), preferred_element_type=F32)


def silu(x):
    return x * (0.5 * jnp.tanh(0.5 * x) + 0.5)


def split3(x):
    hi = x.astype(BF16).astype(F32)
    rest = x - hi
    mid = rest.astype(BF16).astype(F32)
    return jnp.concatenate([hi, mid, rest - mid], axis=0)


def kernel(
    outers,
    chips,
    tok_hbm,
    decay_hbm,
    wq_hbm,
    wk_hbm,
    wv_hbm,
    gain_hbm,
    wo_hbm,
    out_hbm,
    tok,
    decay,
    wq,
    wk,
    wv,
    gain,
    wo,
    q,
    k,
    v,
    cum_b,
    cum_t,
    intra,
    local,
    crossed,
    chip,
    in1,
    prefix,
    total,
    in2,
    out3,
    in3,
    give,
    state,
    f_own,
    f_sib,
    f_chip,
    f_in1,
    normed,
    partial,
    out,
    load_sem,
    store_sem,
    f0_sem,
    f1_sem,
    s0_sem,
    s1_sem,
    s2_sem,
    s3_sem,
    s4_sem,
):
    o = lax.axis_index("outer")
    inner = lax.axis_index("inner")
    z, c = inner // 2, inner % 2
    y, x = o // SIDE, o % SIDE
    sibling = (o, z * 2 + 1 - c)

    def along(d):
        return (z + d) % chips

    def at_z(other):
        return (o, other * 2 + c)

    far_z = sorted(range(1, chips), key=lambda d: -min(d, chips - d))
    near_z = [0] + far_z[::-1]
    plane = sorted(
        ((a, b) for a in range(outers // SIDE) for b in range(SIDE) if (a, b) != (0, 0)),
        key=lambda t: -(min(t[0], outers // SIDE - t[0]) + min(t[1], SIDE - t[1])),
    )

    def group_at(a, b):
        return (y + a) % (outers // SIDE) * SIDE + (x + b) % SIDE

    def load(src, dst, n):
        copy = pltpu.make_async_copy(src, dst, load_sem.at[n])
        copy.start()
        return copy

    mine = z // 2
    odd = z % 2
    order = [(mine + 2) % QUADS, (mine + 1 + 2 * odd) % QUADS, (mine + 3 - 2 * odd) % QUADS, mine]

    load_decay = load(decay_hbm, decay, 0)
    load_tok = load(tok_hbm, tok, 1)
    load_k, load_v, load_q, load_o = [], [], [], []
    for n in range(QUADS):
        cols = pl.ds(pl.multiple_of(order[n] * QUAD, QUAD), QUAD)
        load_k.append(load(wk_hbm.at[:, cols], wk.at[n], 2 + n))
        load_v.append(load(wv_hbm.at[:, cols], wv.at[n], 6 + n))
    for n in range(QUADS):
        load_q.append(load(wq_hbm.at[:, pl.ds(n * QUAD, QUAD)], wq.at[n], 10 + n))
    for n in range(PAIRS):
        load_o.append(load(wo_hbm.at[pl.ds(n * PAIR, PAIR)], wo.at[n], 14 + n))
    load_gain = load(gain_hbm, gain, 22)

    barrier = pltpu.get_barrier_semaphore()
    pl.semaphore_signal(barrier, inc=1, device_id=sibling, device_id_type=MESH)
    for d in range(1, chips):
        pl.semaphore_signal(barrier, inc=1, device_id=at_z(along(d)), device_id_type=MESH)
    for a, b in plane:
        pl.semaphore_signal(
            barrier, inc=1, device_id=(group_at(a, b), inner), device_id_type=MESH
        )

    sent = []

    def remote(src, dst, sems, slot_out, slot_in, device):
        return pltpu.make_async_remote_copy(
            src_ref=src,
            dst_ref=dst,
            send_sem=sems.at[0, slot_out],
            recv_sem=sems.at[1, slot_in],
            device_id=device,
            device_id_type=MESH,
        )

    def send(src, dst, sems, slot_out, slot_in, device):
        copy = remote(src, dst, sems, slot_out, slot_in, device)
        copy.start()
        sent.append(copy)

    def arrived(dst, sems, slot_in):
        remote(dst, dst, sems, slot_in, slot_in, sibling).wait_recv()

    first = lax.broadcasted_iota(jnp.int32, (1, PAIR), 1) < HEAD
    rows = lax.broadcasted_iota(jnp.int32, (TOKENS, TOKENS), 0)
    cols = lax.broadcasted_iota(jnp.int32, (TOKENS, TOKENS), 1)
    triangle = jnp.where(rows <= cols, 1.0, 0.0).astype(BF16)
    load_decay.wait()
    sums = dot(split3(decay[...]).astype(BF16), triangle)
    turned = sums[:HEADS] + (sums[HEADS : 2 * HEADS] + sums[2 * HEADS :])
    for h in range(HEADS):
        cum_t[h] = turned[h : h + 1, :]
    falls = jnp.exp(jnp.broadcast_to(turned[:, TOKENS - 1 :], (HEADS, PAIR)))
    for p in range(PAIRS):
        f_own[p : p + 1, :] = jnp.where(
            first, falls[2 * p : 2 * p + 1], falls[2 * p + 1 : 2 * p + 2]
        )
    padded = jnp.concatenate(
        [split3(turned), jnp.zeros((PAIR - 3 * HEADS, TOKENS), F32)], axis=0
    )
    upright = padded.T.astype(BF16)

    def project_states(n):
        quad = order[n]
        r = lax.broadcasted_iota(jnp.int32, (PAIR, 4 * PAIR), 0)
        s = lax.broadcasted_iota(jnp.int32, (PAIR, 4 * PAIR), 1)
        spread = jnp.where((r % HEADS == quad * 4 + s // PAIR) & (r < 3 * HEADS), 1.0, 0.0)
        cums = dot(upright, spread.astype(BF16))
        keys = silu(dot(tok[...], wk[n])).astype(BF16)
        values = dot(tok[...], wv[n]).astype(BF16)
        for e in range(2):
            p = 2 * quad + e
            part = slice(e * PAIR, (e + 1) * PAIR)
            one = cums[:, 2 * e * PAIR : (2 * e + 1) * PAIR]
            two = cums[:, (2 * e + 1) * PAIR : (2 * e + 2) * PAIR]
            cum_b[2 * p] = one
            cum_b[2 * p + 1] = two
            k[p] = keys[:, part]
            v[p] = values[:, part]
            run = jnp.where(first, one, two)
            left = jnp.exp(run[TOKENS - 1 :, :] - run)
            scaled = (keys[:, part].astype(F32) * left).astype(BF16)
            outer = dot_tn(scaled, values[:, part])
            own = jnp.where(first, outer[:HEAD], outer[HEAD:])
            local[p] = own.reshape(2, HALF, PAIR)

    def send_cross(n):
        two = pl.ds(2 * order[n], 2)
        send(local.at[two, 1 - c], crossed.at[two], s0_sem, n, n, sibling)

    def exchange_falls():
        arrived(f_sib, f0_sem, 0)
        both = f_own[...] * f_sib[...]
        f_chip[...] = both
        f_in1[z] = both
        for d in far_z:
            send(f_chip, f_in1.at[z], f1_sem, d, z, at_z(along(d)))

    def send_chip(n):
        two = pl.ds(2 * order[n], 2)
        arrived(crossed.at[two], s0_sem, n)
        for e in range(2):
            p = 2 * order[n] + e
            own = local[p, c]
            other = crossed[p]
            late = jnp.where(c == 0, f_sib[pl.ds(p, 1), :], f_own[pl.ds(p, 1), :])
            chip[p] = jnp.where(c == 0, late * own + other, late * other + own)
        if n < QUADS - 1:
            for e in range(2):
                p = 2 * order[n] + e
                send(chip.at[p], in1.at[z], s1_sem, 2 * n + e, z, at_z(p))
        else:
            in1[z] = chip[z]
            p = z + 1 - 2 * odd
            send(chip.at[p], in1.at[z], s1_sem, 2 * n, z, at_z(p))

    def project_queries(n):
        load_q[n].wait()
        queries = silu(dot(tok[...], wq[n])).astype(BF16)
        q[2 * n] = queries[:, :PAIR]
        q[2 * n + 1] = queries[:, PAIR:]

    def attend(p):
        for i in range(TOKENS // SUB):
            here = slice(i * SUB, (i + 1) * SUB)
            upto = (i + 1) * SUB
            queries = q[p, here, :]
            nothing = jnp.zeros_like(queries)
            keys = k[p, :upto, :]
            weights = []
            for e in range(2):
                own = (
                    jnp.where(first, queries, nothing)
                    if e == 0
                    else jnp.where(first, nothing, queries)
                )
                scores = dot_nt(own, keys)
                row = cum_b[2 * p + e, here, :]
                for j in range(i + 1):
                    diff = row - cum_t[2 * p + e, :, j * SUB : (j + 1) * SUB]
                    if j == i:
                        r = lax.broadcasted_iota(jnp.int32, (SUB, SUB), 0)
                        s = lax.broadcasted_iota(jnp.int32, (SUB, SUB), 1)
                        diff = jnp.where(s <= r, diff, -jnp.inf)
                    weights.append(
                        (scores[:, j * SUB : (j + 1) * SUB] * jnp.exp(diff)).astype(BF16)
                    )
            values = v[p, :upto, :]
            nothing = jnp.zeros_like(values)
            heads = jnp.concatenate(
                [jnp.where(first, values, nothing), jnp.where(first, nothing, values)], axis=0
            )
            intra[p, here, :] = dot(jnp.concatenate(weights, axis=1), heads)

    load_tok.wait()
    for n in range(QUADS):
        load_k[n].wait()
        load_v[n].wait()
        project_states(n)
        if n == 0:
            pl.semaphore_wait(barrier, chips + outers - 1)
            send(f_own, f_sib, f0_sem, 0, 0, sibling)
        send_cross(n)
        if n == 1:
            exchange_falls()
        if n >= 1:
            send_chip(n - 1)
    project_queries(0)
    send_chip(QUADS - 1)
    for n in range(1, QUADS):
        project_queries(n)
    for p in range(0, 2):
        attend(p)

    for d in near_z[1:]:
        arrived(f_in1.at[along(d)], f1_sem, along(d))
        arrived(in1.at[along(d)], s1_sem, along(d))
    run = jnp.zeros((HALF, PAIR), F32)
    group = jnp.ones((1, PAIR), F32)
    for i in range(chips):
        prefix[i] = run
        fall = f_in1[i, pl.ds(z, 1), :]
        run = fall * run + in1[i]
        group = group * fall
    total[:HALF] = run
    total[HALF:] = jnp.broadcast_to(group, (8, PAIR))
    for n, (a, b) in enumerate(plane):
        other = group_at(a, b)

        @pl.when(other > o)
        def _():
            remote(total, in2.at[o], s2_sem, n, o, (other, inner)).start()

    for p in range(2, 7):
        attend(p)

    def earlier(i, before):
        arrived(in2.at[i], s2_sem, i)
        return in2[i, HALF : HALF + 1, :] * before + in2[i, :HALF, :]

    before = lax.fori_loop(0, o, earlier, jnp.zeros((HALF, PAIR), F32))
    fall = jnp.ones((1, PAIR), F32)
    for i in range(chips):
        out3[i] = fall * before + prefix[i]
        fall = fall * f_in1[i, pl.ds(z, 1), :]
    for d in far_z:
        t = along(d)
        send(out3.at[t], in3.at[z], s3_sem, d, z, at_z(t))
    in3[z] = out3[z]

    for p in range(7, PAIRS):
        attend(p)
    load_gain.wait()
    for n in range(PAIRS):
        load_o[n].wait()

    def enter(d):
        p = along(d)
        if d > 0:
            arrived(in3.at[p], s3_sem, p)
        enters = in3[p]
        first_local = jnp.where(c == 0, local[p, 0], crossed[p])
        fall = jnp.where(c == 0, f_own[pl.ds(p, 1), :], f_sib[pl.ds(p, 1), :])
        middle = fall * enters + first_local
        state[p, c] = jnp.where(c == 0, enters, middle)
        give[p] = jnp.where(c == 0, middle, enters)
        send(give.at[p], state.at[p, c], s4_sem, p, p, sibling)

    r = lax.broadcasted_iota(jnp.int32, (PAIR, PAIR), 0) // HEAD
    s = lax.broadcasted_iota(jnp.int32, (PAIR, PAIR), 1) // HEAD
    means = jnp.where(r == s, 1.0 / HEAD, 0.0).astype(BF16)

    def norm(pairs):
        for p in pairs:
            arrived(state.at[p, 1 - c], s4_sem, p)
        for p in pairs:
            flat = state[p].reshape(HEAD, PAIR)
            both = jnp.concatenate(
                [jnp.where(first, flat, 0.0), jnp.where(first, 0.0, flat)], axis=0
            )
            inter = dot(q[p], both.astype(BF16))
            run = jnp.where(first, cum_b[2 * p], cum_b[2 * p + 1])
            attended = intra[p] + jnp.exp(run) * inter
            mean = dot((attended * attended).astype(BF16), means)
            normed[p] = (attended * lax.rsqrt(mean + 1e-5) * gain[p]).astype(BF16)

    def mix(pairs, n):
        left = jnp.concatenate([normed[p] for p in pairs], axis=1)
        right = jnp.concatenate([wo[p, :, n * QUAD : (n + 1) * QUAD] for p in pairs], axis=0)
        return dot(left, right)

    near = [along(d) for d in near_z[:5]]
    far = [along(d) for d in near_z[5:]]
    for d in near_z[:5]:
        enter(d)
    norm(near)
    for d in near_z[5:]:
        enter(d)
    for n in range(QUADS):
        partial[n] = mix(near, n)
    norm(far)
    stores = []
    for n in range(QUADS):
        out[n] = (partial[n] + mix(far, n)).astype(BF16)
        copy = pltpu.make_async_copy(
            out.at[n], out_hbm.at[:, pl.ds(n * QUAD, QUAD)], store_sem.at[n]
        )
        copy.start()
        stores.append(copy)

    for copy in sent:
        copy.wait_send()
    for n, (a, b) in enumerate(plane):

        @pl.when(group_at(a, b) > o)
        def _():
            remote(total, total, s2_sem, n, n, sibling).wait_send()

    for copy in stores:
        copy.wait()


MESH = pl.DeviceIdType.MESH


def solution(mesh):
    outers, chips = mesh.shape["outer"], mesh.shape["inner"] // 2

    def shards(tokens, log_decay, query_weight, key_weight, value_weight, norm_gain, output_weight):
        vmem = pltpu.VMEM
        dma = pltpu.SemaphoreType.DMA
        weight = vmem((QUADS, WIDTH, QUAD), BF16)
        by_pair = vmem((PAIRS, TOKENS, PAIR), BF16)
        unit = (HALF, PAIR)
        tile = (PAIRS, PAIR)
        return pl.pallas_call(
            functools.partial(kernel, outers, chips),
            out_shape=jax.ShapeDtypeStruct((TOKENS, WIDTH), BF16),
            in_specs=[pl.BlockSpec(memory_space=pl.ANY)] * 7,
            out_specs=pl.BlockSpec(memory_space=pl.ANY),
            scratch_shapes=[
                vmem((TOKENS, WIDTH), BF16),
                vmem((HEADS, TOKENS), F32),
                weight,
                weight,
                weight,
                vmem((PAIRS, 1, PAIR), F32),
                vmem((PAIRS, PAIR, WIDTH), BF16),
                by_pair,
                by_pair,
                by_pair,
                vmem((HEADS, TOKENS, PAIR), F32),
                vmem((HEADS, 1, TOKENS), F32),
                vmem((PAIRS, TOKENS, PAIR), F32),
                vmem((PAIRS, 2) + unit, F32),
                vmem((PAIRS,) + unit, F32),
                vmem((PAIRS,) + unit, F32),
                vmem((chips,) + unit, F32),
                vmem((chips,) + unit, F32),
                vmem((HALF + 8, PAIR), F32),
                vmem((outers, HALF + 8, PAIR), F32),
                vmem((chips,) + unit, F32),
                vmem((PAIRS,) + unit, F32),
                vmem((PAIRS,) + unit, F32),
                vmem((PAIRS, 2) + unit, F32),
                vmem(tile, F32),
                vmem(tile, F32),
                vmem(tile, F32),
                vmem((chips,) + tile, F32),
                by_pair,
                vmem((QUADS, TOKENS, QUAD), F32),
                vmem((QUADS, TOKENS, QUAD), BF16),
                dma((23,)),
                dma((QUADS,)),
                dma((2, 1)),
                dma((2, chips)),
                dma((2, QUADS)),
                dma((2, chips)),
                dma((2, outers)),
                dma((2, chips)),
                dma((2, PAIRS)),
            ],
            compiler_params=pltpu.CompilerParams(
                collective_id=0, has_side_effects=True, vmem_limit_bytes=62 << 20
            ),
            cost_estimate=pl.CostEstimate(
                flops=4 * 10**9, bytes_accessed=10 << 20, transcendentals=2 * 10**6
            ),
        )(
            tokens,
            log_decay.T,
            query_weight,
            key_weight,
            value_weight,
            norm_gain.reshape(PAIRS, 1, PAIR),
            output_weight,
        )

    in_specs = (P(("outer", "inner"), None), P(("outer", "inner"), None), P(), P(), P(), P(), P())
    out_specs = P(("outer", "inner"), None)
    return jax.shard_map(shards, mesh=mesh, in_specs=in_specs, out_specs=out_specs, check_vma=False)
```

time: 48 us -> 35.1 us (0.73)
  Pallas kernels: 41 us -> 32.5 us
  local copies, waits for them, and re-layouts: 6.74 us -> 2.06 us
    pallas_call x1, Pallas kernels: 41 us -> 32.5 us  [shards(): pl.pallas_call(functools.partial(kernel, outers, chips), out_shape=jax.Sh...]
    unnamed x10 -> x1, local copies, waits for them, and re-layouts: 6.74 us -> 2.06 us
where the time goes in v2:
time: 35.1 us; the launch traced here: 34.6 us
  Pallas kernels  32.5 us (93%)
  local copies, waits for them, and re-layouts  2.06 us (6%)
    pallas_call x1, Pallas kernels, shards(): pl.pallas_call(functools.partial(kernel, outers, chips), out_shape=jax.Sh...  32.5 us
    unnamed x1, local copies, waits for them, and re-layouts  2.06 us

profile of v2, /device:TPU:25, one launch (start us, length us, event | category | flops | bytes accessed | tf_op | source)
XLA Modules:
  0.0 34.6 jit_solution(12284996784040984213)
XLA Ops:
  0.0 32.5 %shard_map.73 = bf16[384,1024]{1,0:T(8,128)(2,1)} custom-call(bf16[384,1024]{1,0:T(8,128)(2,1)} %tok_hbm.1, f32[16,384]{1,0:T(8,128)} %bitcast.2, bf16[1024,1024]{1,0:T(8,128)(2,1)} %wq_hbm.1, bf16[1024,1024]{1,0:T(8,128)(2,1)} %wk_hbm.1, bf16[1024,1024]{1,0:T(8,128)(2,1)} %wv_hbm.1, f32[8,1,128]{2,1,0:T(1,128)} %bitcast.3, bf16[1024,1024]{1,0:T(8,128)(2,1)} %wo_hbm.1), custom_call_target="tpu_custom_call" | custom-call | flops 4000000000 | bytes 10485760 | tf_op jit(solution)/shard_map/pallas_call | solution.py:425
  32.5 2.1 %copy.9 = bf16[384,1024]{1,0:T(8,128)(2,1)} copy(bf16[384,1024]{1,0:T(8,128)(2,1)} %shard_map.73) | data formatting | bytes 1572864

commit v3 on v2

--- a/solution.py
+++ b/solution.py
@@ -18,6 +18,7 @@
 TOKENS = 384
 SUB = 128
 WIDTH = 1024
+BARRIER = 2
 SIDE = 4
 HALF = 32
 
@@ -83,14 +84,12 @@
     f_own,
     f_sib,
     f_chip,
-    f_in1,
     normed,
     partial,
     out,
     load_sem,
     store_sem,
     f0_sem,
-    f1_sem,
     s0_sem,
     s1_sem,
     s2_sem,
@@ -130,27 +129,40 @@
 
     load_decay = load(decay_hbm, decay, 0)
     load_tok = load(tok_hbm, tok, 1)
-    load_k, load_v, load_q, load_o = [], [], [], []
-    for n in range(QUADS):
+    load_k, load_v = [], []
+
+    def load_quad(n):
         cols = pl.ds(pl.multiple_of(order[n] * QUAD, QUAD), QUAD)
         load_k.append(load(wk_hbm.at[:, cols], wk.at[n], 2 + n))
         load_v.append(load(wv_hbm.at[:, cols], wv.at[n], 6 + n))
-    for n in range(QUADS):
-        load_q.append(load(wq_hbm.at[:, pl.ds(n * QUAD, QUAD)], wq.at[n], 10 + n))
-    for n in range(PAIRS):
-        load_o.append(load(wo_hbm.at[pl.ds(n * PAIR, PAIR)], wo.at[n], 14 + n))
-    load_gain = load(gain_hbm, gain, 22)
+
+    load_quad(0)
 
     barrier = pltpu.get_barrier_semaphore()
+    for d in far_z:
+        pl.semaphore_signal(barrier, inc=1, device_id=at_z(along(d)), device_id_type=MESH)
     pl.semaphore_signal(barrier, inc=1, device_id=sibling, device_id_type=MESH)
-    for d in range(1, chips):
-        pl.semaphore_signal(barrier, inc=1, device_id=at_z(along(d)), device_id_type=MESH)
+    load_quad(1)
     for a, b in plane:
-        pl.semaphore_signal(
-            barrier, inc=1, device_id=(group_at(a, b), inner), device_id_type=MESH
-        )
+        other = group_at(a, b)
+
+        @pl.when(other < o)
+        def _():
+            pl.semaphore_signal(barrier, inc=1, device_id=(other, inner), device_id_type=MESH)
+
+    for n in range(2, QUADS):
+        load_quad(n)
+
+    load_q = load(wq_hbm, wq, 10)
+    load_o = load(wo_hbm, wo, 11)
+    load_gain = load(gain_hbm, gain, 12)
 
     sent = []
+
+    def settle():
+        for copy in sent:
+            copy.wait_send()
+        sent.clear()
 
     def remote(src, dst, sems, slot_out, slot_in, device):
         return pltpu.make_async_remote_copy(
@@ -219,11 +231,7 @@
 
     def exchange_falls():
         arrived(f_sib, f0_sem, 0)
-        both = f_own[...] * f_sib[...]
-        f_chip[...] = both
-        f_in1[z] = both
-        for d in far_z:
-            send(f_chip, f_in1.at[z], f1_sem, d, z, at_z(along(d)))
+        f_chip[...] = f_own[...] * f_sib[...]
 
     def send_chip(n):
         two = pl.ds(2 * order[n], 2)
@@ -233,7 +241,8 @@
             own = local[p, c]
             other = crossed[p]
             late = jnp.where(c == 0, f_sib[pl.ds(p, 1), :], f_own[pl.ds(p, 1), :])
-            chip[p] = jnp.where(c == 0, late * own + other, late * other + own)
+            chip[p, :HALF] = jnp.where(c == 0, late * own + other, late * other + own)
+            chip[p, HALF:] = jnp.broadcast_to(f_chip[pl.ds(p, 1), :], (8, PAIR))
         if n < QUADS - 1:
             for e in range(2):
                 p = 2 * order[n] + e
@@ -244,8 +253,7 @@
             send(chip.at[p], in1.at[z], s1_sem, 2 * n, z, at_z(p))
 
     def project_queries(n):
-        load_q[n].wait()
-        queries = silu(dot(tok[...], wq[n])).astype(BF16)
+        queries = silu(dot(tok[...], wq[:, n * QUAD : (n + 1) * QUAD])).astype(BF16)
         q[2 * n] = queries[:, :PAIR]
         q[2 * n + 1] = queries[:, PAIR:]
 
@@ -286,14 +294,20 @@
         load_k[n].wait()
         load_v[n].wait()
         project_states(n)
-        if n == 0:
-            pl.semaphore_wait(barrier, chips + outers - 1)
+        if n == BARRIER:
+            pl.semaphore_wait(barrier, chips + outers - 1 - o)
             send(f_own, f_sib, f0_sem, 0, 0, sibling)
-        send_cross(n)
-        if n == 1:
+            for m in range(n):
+                send_cross(m)
+        if n >= BARRIER:
+            send_cross(n)
+        if n == BARRIER + 1:
             exchange_falls()
-        if n >= 1:
+            for m in range(BARRIER):
+                send_chip(m)
+        if n >= BARRIER + 1:
             send_chip(n - 1)
+    load_q.wait()
     project_queries(0)
     send_chip(QUADS - 1)
     for n in range(1, QUADS):
@@ -302,14 +316,13 @@
         attend(p)
 
     for d in near_z[1:]:
-        arrived(f_in1.at[along(d)], f1_sem, along(d))
         arrived(in1.at[along(d)], s1_sem, along(d))
     run = jnp.zeros((HALF, PAIR), F32)
     group = jnp.ones((1, PAIR), F32)
     for i in range(chips):
         prefix[i] = run
-        fall = f_in1[i, pl.ds(z, 1), :]
-        run = fall * run + in1[i]
+        fall = in1[i, HALF : HALF + 1, :]
+        run = fall * run + in1[i, :HALF, :]
         group = group * fall
     total[:HALF] = run
     total[HALF:] = jnp.broadcast_to(group, (8, PAIR))
@@ -320,6 +333,7 @@
         def _():
             remote(total, in2.at[o], s2_sem, n, o, (other, inner)).start()
 
+    settle()
     for p in range(2, 7):
         attend(p)
 
@@ -331,7 +345,7 @@
     fall = jnp.ones((1, PAIR), F32)
     for i in range(chips):
         out3[i] = fall * before + prefix[i]
-        fall = fall * f_in1[i, pl.ds(z, 1), :]
+        fall = fall * in1[i, HALF : HALF + 1, :]
     for d in far_z:
         t = along(d)
         send(out3.at[t], in3.at[z], s3_sem, d, z, at_z(t))
@@ -339,9 +353,15 @@
 
     for p in range(7, PAIRS):
         attend(p)
+    settle()
+    for n, (a, b) in enumerate(plane):
+
+        @pl.when(group_at(a, b) > o)
+        def _():
+            remote(total, total, s2_sem, n, n, sibling).wait_send()
+
     load_gain.wait()
-    for n in range(PAIRS):
-        load_o[n].wait()
+    load_o.wait()
 
     def enter(d):
         p = along(d)
@@ -378,12 +398,12 @@
         right = jnp.concatenate([wo[p, :, n * QUAD : (n + 1) * QUAD] for p in pairs], axis=0)
         return dot(left, right)
 
-    near = [along(d) for d in near_z[:5]]
-    far = [along(d) for d in near_z[5:]]
-    for d in near_z[:5]:
+    near = [along(d) for d in near_z[:6]]
+    far = [along(d) for d in near_z[6:]]
+    for d in near_z[:6]:
         enter(d)
     norm(near)
-    for d in near_z[5:]:
+    for d in near_z[6:]:
         enter(d)
     for n in range(QUADS):
         partial[n] = mix(near, n)
@@ -397,14 +417,7 @@
         copy.start()
         stores.append(copy)
 
-    for copy in sent:
-        copy.wait_send()
-    for n, (a, b) in enumerate(plane):
-
-        @pl.when(group_at(a, b) > o)
-        def _():
-            remote(total, total, s2_sem, n, n, sibling).wait_send()
-
+    settle()
     for copy in stores:
         copy.wait()
 
@@ -430,7 +443,7 @@
             scratch_shapes=[
                 vmem((TOKENS, WIDTH), BF16),
                 vmem((HEADS, TOKENS), F32),
-                weight,
+                vmem((WIDTH, WIDTH), BF16),
                 weight,
                 weight,
                 vmem((PAIRS, 1, PAIR), F32),
@@ -443,8 +456,8 @@
                 vmem((PAIRS, TOKENS, PAIR), F32),
                 vmem((PAIRS, 2) + unit, F32),
                 vmem((PAIRS,) + unit, F32),
-                vmem((PAIRS,) + unit, F32),
-                vmem((chips,) + unit, F32),
+                vmem((PAIRS, HALF + 8, PAIR), F32),
+                vmem((chips, HALF + 8, PAIR), F32),
                 vmem((chips,) + unit, F32),
                 vmem((HALF + 8, PAIR), F32),
                 vmem((outers, HALF + 8, PAIR), F32),
@@ -455,14 +468,12 @@
                 vmem(tile, F32),
                 vmem(tile, F32),
                 vmem(tile, F32),
-                vmem((chips,) + tile, F32),
                 by_pair,
                 vmem((QUADS, TOKENS, QUAD), F32),
                 vmem((QUADS, TOKENS, QUAD), BF16),
-                dma((23,)),
+                dma((13,)),
                 dma((QUADS,)),
                 dma((2, 1)),
-                dma((2, chips)),
                 dma((2, QUADS)),
                 dma((2, chips)),
                 dma((2, outers)),
@@ -482,7 +493,7 @@
             key_weight,
             value_weight,
             norm_gain.reshape(PAIRS, 1, PAIR),
-            output_weight,
+            output_weight.reshape(PAIRS, PAIR, WIDTH),
         )
 
     in_specs = (P(("outer", "inner"), None), P(("outer", "inner"), None), P(), P(), P(), P(), P())

time: 35.1 us -> 34.1 us (0.972); the launches traced: 34.6 us -> 34 us
  Pallas kernels: 32.5 us -> 31.9 us
    pallas_call x1, Pallas kernels: 32.5 us -> 31.9 us  [shards(): pl.pallas_call(functools.partial(kernel, outers, chips), out_shape=jax.Sh...]
where the time goes in v3:
time: 34.1 us; the launch traced here: 34 us
  Pallas kernels  31.9 us (94%)
  local copies, waits for them, and re-layouts  2.06 us (6%)
    pallas_call x1, Pallas kernels, shards(): pl.pallas_call(functools.partial(kernel, outers, chips), out_shape=jax.Sh...  31.9 us
    unnamed x1, local copies, waits for them, and re-layouts  2.06 us

profile of v3, /device:TPU:25, one launch (start us, length us, event | category | flops | bytes accessed | tf_op | source)
XLA Modules:
  0.0 34.0 jit_solution(8756836397747822287)
XLA Ops:
  0.0 31.9 %shard_map.73 = bf16[384,1024]{1,0:T(8,128)(2,1)} custom-call(bf16[384,1024]{1,0:T(8,128)(2,1)} %tok_hbm.1, f32[16,384]{1,0:T(8,128)} %bitcast.4, bf16[1024,1024]{1,0:T(8,128)(2,1)} %wq_hbm.1, bf16[1024,1024]{1,0:T(8,128)(2,1)} %wk_hbm.1, bf16[1024,1024]{1,0:T(8,128)(2,1)} %wv_hbm.1, f32[8,1,128]{2,1,0:T(1,128)} %bitcast.5, bf16[8,128,1024]{2,1,0:T(8,128)(2,1)} %bitcast.3), custom_call_target="tpu_custom_call" | custom-call | flops 4000000000 | bytes 10485760 | tf_op jit(solution)/shard_map/pallas_call | solution.py:438
  31.9 2.1 %copy.9 = bf16[384,1024]{1,0:T(8,128)(2,1)} copy(bf16[384,1024]{1,0:T(8,128)(2,1)} %shard_map.73) | data formatting | bytes 1572864

commit v4 on v3

--- a/solution.py
+++ b/solution.py
@@ -127,6 +127,10 @@
     odd = z % 2
     order = [(mine + 2) % QUADS, (mine + 1 + 2 * odd) % QUADS, (mine + 3 - 2 * odd) % QUADS, mine]
 
+    barrier = pltpu.get_barrier_semaphore()
+    for d in far_z:
+        pl.semaphore_signal(barrier, inc=1, device_id=at_z(along(d)), device_id_type=MESH)
+    pl.semaphore_signal(barrier, inc=1, device_id=sibling, device_id_type=MESH)
     load_decay = load(decay_hbm, decay, 0)
     load_tok = load(tok_hbm, tok, 1)
     load_k, load_v = [], []
@@ -138,10 +142,6 @@
 
     load_quad(0)
 
-    barrier = pltpu.get_barrier_semaphore()
-    for d in far_z:
-        pl.semaphore_signal(barrier, inc=1, device_id=at_z(along(d)), device_id_type=MESH)
-    pl.semaphore_signal(barrier, inc=1, device_id=sibling, device_id_type=MESH)
     load_quad(1)
     for a, b in plane:
         other = group_at(a, b)

time: 34.1 us -> 34.1 us (level)
  no operation moved by 1% of the time
where the time goes in v4:
time: 34.1 us; the launch traced here: 34 us
  Pallas kernels  31.9 us (94%)
  local copies, waits for them, and re-layouts  2.06 us (6%)
    pallas_call x1, Pallas kernels, shards(): pl.pallas_call(functools.partial(kernel, outers, chips), out_shape=jax.Sh...  31.9 us
    unnamed x1, local copies, waits for them, and re-layouts  2.06 us

profile of v4, /device:TPU:25, one launch (start us, length us, event | category | flops | bytes accessed | tf_op | source)
XLA Modules:
  0.0 34.0 jit_solution(16609416914971561380)
XLA Ops:
  0.0 31.9 %shard_map.73 = bf16[384,1024]{1,0:T(8,128)(2,1)} custom-call(bf16[384,1024]{1,0:T(8,128)(2,1)} %tok_hbm.1, f32[16,384]{1,0:T(8,128)} %bitcast.4, bf16[1024,1024]{1,0:T(8,128)(2,1)} %wq_hbm.1, bf16[1024,1024]{1,0:T(8,128)(2,1)} %wk_hbm.1, bf16[1024,1024]{1,0:T(8,128)(2,1)} %wv_hbm.1, f32[8,1,128]{2,1,0:T(1,128)} %bitcast.5, bf16[8,128,1024]{2,1,0:T(8,128)(2,1)} %bitcast.3), custom_call_target="tpu_custom_call" | custom-call | flops 4000000000 | bytes 10485760 | tf_op jit(solution)/shard_map/pallas_call | solution.py:438
  31.9 2.1 %copy.9 = bf16[384,1024]{1,0:T(8,128)(2,1)} copy(bf16[384,1024]{1,0:T(8,128)(2,1)} %shard_map.73) | data formatting | bytes 1572864
